TPU v7x, 32 devices: a whole 2x2x4 slice. The times are simulated.
32 devices in a mesh: req: 16 (over z, y, core), tp: 2 (over x).
Axes of the slice: x: 2, y: 2, z: 4, core: 2. Of those that a mesh axis runs over, the one named last changes fastest.
Arguments:
- hidden: bfloat16 [64, 128, 2048], P('tp', 'req'), may hold values from -6 to 6
- norm_gain: float32 [2048], replicated, may hold values from 0.1 to 1.9
- w_query: bfloat16 [2048, 2048], P(None, 'tp'), may hold values from -0.45335272 to 0.45335272
- w_keyval: bfloat16 [2048, 4, 128], replicated, may hold values from -0.45335272 to 0.45335272
- w_out: bfloat16 [2048, 2048], P('tp'), may hold values from -0.25 to 0.25
- kv_pool: bfloat16 [1024, 256, 4, 128], P('req'), may hold values from -10 to 10
- cache_len: int32 [128], P('req'), may hold values from 1 to 4096, as said below
- draft_count: int32 [128], P('req'), may hold values from 32 to 64, as said below
- parents: int32 [128, 64], P('req'), may hold values from 0 to 62, as said below
Outputs:
- attended: bfloat16 [64, 128, 2048], P('tp', 'req')
Inputs may be any that keep to these rules, and one draw needn't show every extreme that they name: `cache_len`: some request has exactly 4096. `draft_count`: some request has exactly 64. parents[r, t] < t for t >= 1 and parents[r, 0] = 0.
All inputs are finite; a program needn't handle non-finite values.
Results may differ from a plain program's by a relative error of at most 0.035.
Values may be sent and summed in bfloat16 or wider, within the bound.
A program may use at most 192 MiB of HBM per device.

v0:
```python
import functools
import math

import jax
import jax.numpy as jnp
from jax import lax
from jax.experimental import pallas as pl
from jax.experimental.pallas import tpu as pltpu
from jax.sharding import PartitionSpec as P

HQ = 32
KVH = 4
W = 2048


eps = 1e-05
rope_base = 10000.0
hidden_score = -1e30


def ancestry(parents):
    draft_len = parents.shape[-1]
    row_ids = lax.broadcasted_iota(jnp.int32, (draft_len, draft_len), 0)
    col_ids = lax.broadcasted_iota(jnp.int32, (draft_len, draft_len), 1)
    link_mask = jnp.logical_and(parents[..., :, None] == col_ids, row_ids > 0)
    reached = jnp.logical_or(link_mask, row_ids == col_ids).astype(jnp.bfloat16)
    for doubling in range(max(1, (draft_len - 1).bit_length())):
        reached = (
            jnp.einsum("...ts,...su->...tu", reached, reached, preferred_element_type=jnp.float32)
            > 0.5
        ).astype(jnp.bfloat16)
    reached = reached.astype(jnp.float32)
    depths = (jnp.sum(reached, axis=-1) - 1.0).astype(jnp.int32)
    return (reached > 0.5, depths)


def rotate(vectors, cos_part, sin_part):
    half_dim = vectors.shape[-1] // 2
    front_half = vectors[..., :half_dim]
    back_half = vectors[..., half_dim:]
    return jnp.concatenate(
        [
            front_half * cos_part - back_half * sin_part,
            back_half * cos_part + front_half * sin_part,
        ],
        axis=-1,
    )


def attend_kernel(
    page_count, owners, groups_at_once, me_ref, q_ref, kv_ref, dkv_ref, first_ref, tree_ref, out_ref
):
    request = pl.program_id(0)
    head = pl.program_id(1)
    in_copy = lax.rem(request, owners // page_count)
    me = me_ref[0]
    draft_len = first_ref.shape[1]
    page_len = kv_ref.shape[3]
    width = kv_ref.shape[4]
    head_dim = width // 2
    rows = groups_at_once * draft_len
    contract_last = (((1,), (1,)), ((), ()))
    first = first_ref[0]
    slot = lax.broadcasted_iota(jnp.int32, (draft_len, page_len), 1)
    lane = lax.broadcasted_iota(jnp.int32, (page_len, width), 1)
    lane_draft = lax.broadcasted_iota(jnp.int32, (draft_len, width), 1)
    one = jnp.ones((), jnp.bfloat16)
    pages = [
        lax.rem(me + in_copy * page_count + page, owners) for page in range(page_count)
    ]

    def part(step, carry):
        here = pl.ds(pl.multiple_of(step * rows, rows), rows)
        q = q_ref[0, 0, here, :]
        tree_bias = jnp.concatenate([tree_ref[0]] * groups_at_once, axis=0)
        tree_scores = (
            lax.dot_general(
                q, dkv_ref[0, 0], contract_last, preferred_element_type=jnp.float32
            )
            + tree_bias
        )
        top = jnp.max(tree_scores, axis=-1, keepdims=True)
        scores = []
        tops = None
        for page in range(page_count):
            bias = jnp.where(slot + page * page_len >= first, 0.0, hidden_score)
            found = lax.dot_general(
                q, kv_ref[pages[page], 0, head], contract_last, preferred_element_type=jnp.float32
            ) + jnp.concatenate([bias] * groups_at_once, axis=0)
            scores.append(found)
            tops = found if tops is None else jnp.maximum(tops, found)
        top = jnp.maximum(top, jnp.max(tops, axis=-1, keepdims=True))
        weights = jnp.exp(tree_scores - top).astype(jnp.bfloat16)
        total = jnp.dot(
            weights,
            jnp.where(lane_draft < head_dim, one, dkv_ref[0, 0]),
            preferred_element_type=jnp.float32,
        )
        for page in range(page_count):
            weights = jnp.exp(scores[page] - top).astype(jnp.bfloat16)
            total = total + jnp.dot(
                weights,
                jnp.where(lane < head_dim, one, kv_ref[pages[page], 0, head]),
                preferred_element_type=jnp.float32,
            )
        mixed = (total[:, head_dim:] / total[:, :1]).astype(jnp.bfloat16)
        columns = groups_at_once * head_dim
        out_ref[0, :, pl.ds(pl.multiple_of(step * columns, columns), columns)] = jnp.concatenate(
            [mixed[g * draft_len : (g + 1) * draft_len] for g in range(groups_at_once)], axis=1
        )
        return carry

    lax.fori_loop(0, q_ref.shape[2] // rows, part, 0)


def attend(me, q, kv, draft_kv, first, tree_bias, page_count):
    count, kv_count, rows, width = q.shape
    owners = kv.shape[0]
    draft_len = first.shape[1]
    slots = page_count * kv.shape[3] + draft_len
    chunk_req = owners // page_count
    columns = rows // draft_len * (width // 2)
    groups_at_once = math.gcd(rows // draft_len, 4)
    return pl.pallas_call(
        functools.partial(attend_kernel, page_count, owners, groups_at_once),
        grid=(count, kv_count),
        in_specs=[
            pl.BlockSpec(memory_space=pltpu.SMEM),
            pl.BlockSpec((1, 1, rows, width), lambda r, c: (r, c, 0, 0)),
            pl.BlockSpec(
                (owners, 1) + kv.shape[2:], lambda r, c: (0, r // chunk_req, 0, 0, 0)
            ),
            pl.BlockSpec((1, 1, draft_len, width), lambda r, c: (r, c, 0, 0)),
            pl.BlockSpec((1, draft_len, 1), lambda r, c: (r, 0, 0)),
            pl.BlockSpec((1, draft_len, draft_len), lambda r, c: (r, 0, 0)),
        ],
        out_specs=pl.BlockSpec((1, draft_len, columns), lambda r, c: (r, 0, c)),
        out_shape=jax.ShapeDtypeStruct((count, draft_len, kv_count * columns), jnp.bfloat16),
        compiler_params=pltpu.CompilerParams(vmem_limit_bytes=32 * 1024 * 1024),
        cost_estimate=pl.CostEstimate(
            flops=count * kv_count * rows * slots * width * 4,
            bytes_accessed=kv.size * 2 + q.size * 4,
            transcendentals=count * kv_count * rows * slots,
        ),
    )(me, q, kv, draft_kv, first, tree_bias)


def per_device(
    hidden, norm_gain, w_query, w_keyval, w_out, kv_pool, cache_len, draft_count, parents
):
    req_dev = cache_len.shape[0]
    draft_len = parents.shape[1]
    d_model = hidden.shape[2]
    head_dim = w_keyval.shape[2] // 2
    heads_here = w_query.shape[1] // head_dim
    kv_count = max(1, heads_here // (HQ // KVH))
    group_size = heads_here // kv_count
    my_tp = lax.axis_index("tp")
    kv_first = my_tp * heads_here // (HQ // KVH)
    page_len = kv_pool.shape[1]
    page_count = W // page_len
    owners = lax.axis_size("req")
    capacity = req_dev * page_count // owners
    chunk_req = owners // page_count
    me = lax.axis_index("req").astype(jnp.int32).reshape(1)
    query_width = heads_here * head_dim
    tp = lax.axis_size("tp")
    pair = tp == 2
    swap = [(0, 1), (1, 0)]

    by_head = kv_pool.transpose(0, 2, 1, 3)
    by_head = by_head.reshape((owners, capacity) + by_head.shape[1:])
    cuts = [0, capacity - 1, capacity] if capacity > 1 else [0, capacity]
    spans = list(zip(cuts[:-1], cuts[1:]))
    outgoing = [
        lax.dynamic_slice(
            by_head,
            (0, start, kv_first, 0, 0),
            (owners, stop - start, kv_count) + by_head.shape[3:],
        )
        for start, stop in spans
    ]

    def exchange(pages):
        return lax.all_to_all(pages, "req", split_axis=0, concat_axis=0, tiled=True)

    first_out, hidden, w_keyval, parents, cache_len = lax.optimization_barrier(
        (outgoing[0], hidden, w_keyval, parents, cache_len)
    )
    windows = [exchange(first_out)]

    w_kv_mine = lax.dynamic_slice_in_dim(w_keyval, kv_first, kv_count, 1).reshape(
        d_model, kv_count * 2 * head_dim
    )
    w_both = jnp.concatenate([w_query, w_kv_mine], axis=1)
    if pair:
        inputs = jnp.concatenate([hidden, lax.ppermute(hidden, "tp", swap)], axis=0)
    else:
        inputs = lax.all_gather(hidden, "tp", axis=0, tiled=True)
    inputs = inputs.astype(jnp.float32)

    def held(entries, axis):
        if not pair:
            return entries
        return jnp.where(my_tp == 0, entries, jnp.roll(entries, draft_len // 2, axis))

    normed = (
        inputs * lax.rsqrt(jnp.mean(inputs * inputs, axis=-1, keepdims=True) + eps) * norm_gain
    ).astype(jnp.bfloat16)
    projected = jnp.einsum("trd,de->tre", normed, w_both, preferred_element_type=jnp.float32)
    reached, depths = ancestry(parents)
    reached = held(held(reached, 1), 2)
    depths = held(depths, 1)
    position = (cache_len[:, None] + depths).T
    frequency = jnp.exp(
        jnp.arange(head_dim // 2, dtype=jnp.float32) * (-2.0 * math.log(rope_base) / head_dim)
    )
    angles = position.astype(jnp.float32)[..., None, None] * frequency
    cos_part = jnp.cos(angles)
    sin_part = jnp.sin(angles)
    queries = rotate(
        projected[..., :query_width].reshape(draft_len, req_dev, heads_here, head_dim),
        cos_part,
        sin_part,
    )
    queries = (queries * head_dim ** (-0.5)).astype(jnp.bfloat16)
    queries = queries.reshape(draft_len, req_dev, kv_count, group_size, head_dim)
    queries = queries.transpose(1, 2, 3, 0, 4).reshape(
        req_dev, kv_count, group_size * draft_len, head_dim
    )
    queries = jnp.pad(queries, ((0, 0), (0, 0), (0, 0), (0, head_dim)))
    keyvals = projected[..., query_width:].reshape(draft_len, req_dev, kv_count, 2 * head_dim)
    draft_kv = jnp.concatenate(
        [rotate(keyvals[..., :head_dim], cos_part, sin_part), keyvals[..., head_dim:]], axis=-1
    ).astype(jnp.bfloat16)
    draft_kv = draft_kv.transpose(1, 2, 0, 3)
    tree_bias = jnp.where(reached, 0.0, hidden_score)
    first_slot = jnp.maximum(W - cache_len[:, None], depths + 1)[..., None]
    slots = held(jnp.arange(draft_len, dtype=jnp.int32), 0)
    valid_rows = slots[:, None] < draft_count[None, :]

    if len(spans) > 1:
        last, windows[0], queries, draft_kv, first_slot, tree_bias = lax.optimization_barrier(
            (outgoing[1], windows[0], queries, draft_kv, first_slot, tree_bias)
        )
        windows.append(exchange(last))

    results = []
    for window, (start, stop) in zip(windows, spans):
        here = slice(start * chunk_req, stop * chunk_req)
        mixed = attend(
            me,
            queries[here],
            window,
            draft_kv[here],
            first_slot[here],
            tree_bias[here],
            page_count,
        )
        term = jnp.einsum("rth,hd->rtd", mixed, w_out, preferred_element_type=jnp.float32)
        if pair:
            half = draft_len // 2
            other = lax.ppermute(term[:, half:].astype(jnp.bfloat16), "tp", swap)
            total = term[:, :half] + other.astype(jnp.float32)
            keep = valid_rows[:half, here].T[..., None]
            results.append(jnp.where(keep, total, 0.0).astype(jnp.bfloat16))
        else:
            keep = valid_rows[:, here].T[..., None]
            results.append(jnp.where(keep, term, 0.0).astype(jnp.bfloat16))
    result = jnp.concatenate(results, axis=0).transpose(1, 0, 2)
    if pair:
        return result
    return lax.psum_scatter(result, "tp", scatter_dimension=0, tiled=True)


def solution(mesh):
    in_specs = (
        P("tp", "req", None),
        P(),
        P(None, "tp"),
        P(),
        P("tp", None),
        P("req", None, None, None),
        P("req"),
        P("req"),
        P("req", None),
    )
    out_specs = P("tp", "req", None)
    return jax.shard_map(
        per_device, mesh=mesh, in_specs=in_specs, out_specs=out_specs, check_vma=False
    )
```

profile of v0, /device:TPU:13, one launch (start us, length us, event | category | flops | bytes accessed | tf_op | source)
XLA Modules:
  0.0 238.3 jit_solution(1032501442264591318)
XLA Ops:
  0.0 15.1 %copy.97 = bf16[64,4,256,128]{3,2,1,0:T(8,128)(2,1)} copy(bf16[64,4,256,128]{3,1,2,0:T(4,128)(2,1)} %bitcast.50) | data formatting | bytes 33554432 | tf_op jit(solution)/shard_map/transpose | solution.py:171
  15.1 6.2 %constant_dynamic-slice_fusion.1 = bf16[16,3,2,256,128]{4,3,2,1,0:T(8,128)(2,1)} fusion(bf16[16,4,4,256,128]{4,3,2,1,0:T(8,128)(2,1)} %bitcast.48, s32[]{:T(128)S(6)} %select_n.68), kind=kLoop, calls=%fused_computation.104 | loop fusion | bytes 12582916 | tf_op jit(solution)/shard_map/dynamic_slice | solution.py:176
  21.4 6.6 %all-to-all-start = ((bf16[16,3,2,256,128]{4,3,2,1,0:T(8,128)(2,1)}), bf16[16,3,2,256,128]{4,3,2,1,0:T(8,128)(2,1)}, u32[]{:S(2)}, u32[]{:S(2)}) async-start(bf16[16,3,2,256,128]{4,3,2,1,0:T(8,128)(2,1)} %constant_dynamic-slice_fusion.1), calls=%async_computation | async-start | bytes 12582912 | tf_op jit(solution)/shard_map/all_to_all | solution.py:185
  27.9 1.2 collective-permute-start
  29.1 3.0 %copy.100 = bf16[2048,4,128]{0,2,1:T(8,128)(2,1)S(1)} copy(bf16[2048,4,128]{2,1,0:T(4,128)(2,1)} %param.12) | data formatting | bytes 4194304 | tf_op jit(solution)/shard_map/optimization_barrier | solution.py:187
  32.1 0.1 constant_dynamic-slice_fusion
  32.3 0.5 copy.101
  32.8 0.3 fusion.39
  33.2 0.2 fusion.38
  33.5 0.2 fusion.37
  33.8 0.2 fusion.36
  34.0 0.2 fusion.35
  34.3 0.2 fusion.34
  34.5 0.1 convert_reduce_fusion
  34.7 0.1 slice_bitcast_fusion.4
  34.7 0.1 fusion.62
  34.8 1.0 multiply_cosine_fusion
  35.8 0.2 copy.105
  36.0 0.2 copy.104
  36.1 0.1 copy.111
  36.3 0.1 pad_add_fusion
  36.4 0.2 copy.112
  36.5 0.1 convert_compare_fusion
  36.6 3.2 %constant_dynamic-slice_fusion.2 = bf16[16,1,2,256,128]{4,3,2,1,0:T(8,128)(2,1)} fusion(bf16[16,4,4,256,128]{4,3,2,1,0:T(8,128)(2,1)} %bitcast.49, s32[]{:T(128)S(6)} %select_n.68), kind=kLoop, calls=%fused_computation.105 | loop fusion | bytes 4194308 | tf_op jit(solution)/shard_map/dynamic_slice | solution.py:176
  39.8 0.1 add_select_fusion
  39.9 0.1 fusion.66
  40.1 0.1 fusion.56
  40.2 0.8 add_maximum_fusion
  41.0 11.6 %collective-permute-done = bf16[32,8,2048]{2,1,0:T(8,128)(2,1)} collective-permute-done((bf16[32,8,2048]{2,1,0:T(8,128)(2,1)}, bf16[32,8,2048]{2,1,0:T(8,128)(2,1)}, u32[]{:S(2)}, u32[]{:S(2)}) %collective-permute-start) | collective-permute-done | bytes 1048608 | tf_op jit(solution)/shard_map/ppermute | solution.py:197
  52.6 2.0 fusion.3
  54.7 0.1 copy.99
  54.8 5.8 %fusion = f32[64,8,1280]{2,1,0:T(8,128)S(1)} fusion(bf16[2048,256]{1,0:T(8,128)(2,1)S(1)} %copy.101, bf16[2048,1024]{1,0:T(8,128)(2,1)} %param.11, f32[2048]{0:T(1024)S(1)} %copy-done.9, f32[64,8]{1,0:T(8,128)S(1)} %copy.99, bf16[32,8,2048]{2,1,0:T(8,128)(2,1)} %collective-permute-done, bf16[32,8,2048]{2,1,0:T(8,128)(2,1)} %param.9), kind=kOutput, calls=%fused_computation.3 | convolution fusion | flops 2700083200 | bytes 9971712 | tf_op jit(solution)/shard_map/trd,de->tre/dot_general | solution.py:210
  60.6 1.5 copy-done.2
  62.1 0.3 slice.130
  62.4 2.5 %reshape.153 = f32[64,8,16,64]{3,2,1,0:T(8,128)} reshape(f32[64,8,1024]{2,1,0:T(8,128)S(1)} %slice.130) | data formatting | bytes 4194304 | tf_op jit(solution)/shard_map/reshape | solution.py:222
  64.9 4.7 %multiply_subtract_fusion = (f32[64,8,16,32]{3,2,1,0:T(8,128)S(1)}, f32[64,8,16,32]{3,2,1,0:T(8,128)S(1)}) fusion(f32[64,8,16,64]{3,2,1,0:T(8,128)} %reshape.153, f32[64,8,32]{2,1,0:T(8,128)S(1)} %copy.105, f32[64,8,32]{2,1,0:T(8,128)S(1)} %copy.104), kind=kLoop, calls=%fused_computation.16 | loop fusion | flops 1572864 | bytes 4325376 | tf_op jit(solution)/shard_map/sub | solution.py:43
  69.7 2.4 %copy.107 = f32[64,8,16,32]{3,0,2,1:T(8,128)S(1)} copy(f32[64,8,16,32]{3,2,1,0:T(8,128)S(1)} %get-tuple-element.28) | data formatting | bytes 2097152 | tf_op jit(solution)/shard_map/add | solution.py:44
  72.1 2.4 %copy.106 = f32[64,8,16,32]{3,0,2,1:T(8,128)S(1)} copy(f32[64,8,16,32]{3,2,1,0:T(8,128)S(1)} %get-tuple-element.27) | data formatting | bytes 2097152 | tf_op jit(solution)/shard_map/sub | solution.py:43
  74.6 1.1 slice_bitcast_fusion
  75.6 0.1 slice.136
  75.9 1.2 fusion.6
  77.0 1.9 pad.4
  79.0 0.2 fusion.65
  79.2 0.4 subtract_convert_fusion
  79.6 0.3 maximum_bitcast_fusion.3
  79.8 85.5 %all-to-all-done.kv_ref = bf16[16,3,2,256,128]{4,3,2,1,0:T(8,128)(2,1)} async-done(((bf16[16,3,2,256,128]{4,3,2,1,0:T(8,128)(2,1)}), bf16[16,3,2,256,128]{4,3,2,1,0:T(8,128)(2,1)}, u32[]{:S(2)}, u32[]{:S(2)}) %all-to-all-start) | async-done | bytes 6291488 | tf_op jit(solution)/shard_map/all_to_all | solution.py:185
  165.3 4.9 %all-to-all-start.1 = ((bf16[16,1,2,256,128]{4,3,2,1,0:T(8,128)(2,1)}), bf16[16,1,2,256,128]{4,3,2,1,0:T(8,128)(2,1)S(1)}, u32[]{:S(2)}, u32[]{:S(2)}) async-start(bf16[16,1,2,256,128]{4,3,2,1,0:T(8,128)(2,1)} %constant_dynamic-slice_fusion.2), calls=%async_computation.1 | async-start | bytes 4194304 | tf_op jit(solution)/shard_map/all_to_all | solution.py:185
  170.3 0.1 broadcast_select_fusion
  170.5 1.5 slice.117.q_ref
  172.1 30.7 %shard_map.91 = bf16[6,64,1024]{2,1,0:T(8,128)(2,1)S(1)} custom-call(s32[1]{0:T(128)} %bitcast.1.me_ref, bf16[6,2,512,128]{3,2,1,0:T(8,128)(2,1)S(1)} %slice.117.q_ref, bf16[16,3,2,256,128]{4,3,2,1,0:T(8,128)(2,1)} %all-to-all-done.kv_ref, bf16[6,2,64,128]{3,2,1,0:T(8,128)(2,1)S(1)} %slice.118.dkv_ref, s32[6,64,1]{2,1,0:T(8,128)S(1)} %slice.119.first_ref, ...), custom_call_target="tpu_custom_call" | custom-call | flops 6643777536 | bytes 9437184 | tf_op jit(solution)/shard_map/pallas_call | solution.py:124
  202.8 1.8 fusion.9
  204.6 1.1 slice.166
  205.7 1.2 collective-permute-start.1
  207.0 1.1 slice.124.q_ref
  208.0 0.8 slice.125.dkv_ref
  208.9 9.1 %all-to-all-done.1.kv_ref = bf16[16,1,2,256,128]{4,3,2,1,0:T(8,128)(2,1)S(1)} async-done(((bf16[16,1,2,256,128]{4,3,2,1,0:T(8,128)(2,1)}), bf16[16,1,2,256,128]{4,3,2,1,0:T(8,128)(2,1)S(1)}, u32[]{:S(2)}, u32[]{:S(2)}) %all-to-all-start.1) | async-done | bytes 2097184 | tf_op jit(solution)/shard_map/all_to_all | solution.py:185
  218.1 9.5 %shard_map.92 = bf16[2,64,1024]{2,1,0:T(8,128)(2,1)S(1)} custom-call(s32[1]{0:T(128)} %bitcast.1.me_ref, bf16[2,2,512,128]{3,2,1,0:T(8,128)(2,1)S(1)} %slice.124.q_ref, bf16[16,1,2,256,128]{4,3,2,1,0:T(8,128)(2,1)S(1)} %all-to-all-done.1.kv_ref, bf16[2,2,64,128]{3,2,1,0:T(8,128)(2,1)S(1)} %slice.125.dkv_ref, s32[2,64,1]{2,1,0:T(8,128)S(1)} %slice.126.first_ref, ...), custom_call_target="tpu_custom_call" | custom-call | flops 2214592512 | bytes 3145728 | tf_op jit(solution)/shard_map/pallas_call | solution.py:124
  227.6 0.7 fusion.7
  228.4 1.3 collective-permute-start.2
  229.7 1.4 fusion.15
  231.1 5.5 %collective-permute-done.2 = bf16[2,32,2048]{2,1,0:T(8,128)(2,1)S(1)} collective-permute-done((bf16[2,32,2048]{2,1,0:T(8,128)(2,1)S(1)}, bf16[2,32,2048]{2,1,0:T(8,128)(2,1)S(1)}, u32[]{:S(2)}, u32[]{:S(2)}) %collective-permute-start.2) | collective-permute-done | bytes 262176 | tf_op jit(solution)/shard_map/ppermute | solution.py:263
  236.5 0.1 fusion.41
  236.6 0.1 maximum_bitcast_fusion.2
  236.7 1.5 copy.113
  (48 shorter events, 0.8 us)
Async XLA Ops:
  21.4 144.0 %all-to-all-start = ((bf16[16,3,2,256,128]{4,3,2,1,0:T(8,128)(2,1)}), bf16[16,3,2,256,128]{4,3,2,1,0:T(8,128)(2,1)}, u32[]{:S(2)}, u32[]{:S(2)}) async-start(bf16[16,3,2,256,128]{4,3,2,1,0:T(8,128)(2,1)} %constant_dynamic-slice_fusion.1), calls=%async_computation | async-start | bytes 12582912 | tf_op jit(solution)/shard_map/all_to_all | solution.py:185
  27.9 24.7 %collective-permute-start = (bf16[32,8,2048]{2,1,0:T(8,128)(2,1)}, bf16[32,8,2048]{2,1,0:T(8,128)(2,1)}, u32[]{:S(2)}, u32[]{:S(2)}) collective-permute-start(bf16[32,8,2048]{2,1,0:T(8,128)(2,1)} %param.9), channel_id=1, source_target_pairs={{0,1},{1,0},{2,3},{3,2},{4,5},{5,4},{6,7},{7,6},{8,9},{9,8},{10,11... | collective-permute-start | bytes 3145736 | tf_op jit(solution)/shard_map/ppermute | solution.py:197
  29.1 3.7 %copy-start.10 = (s32[8,64]{1,0:T(8,128)S(1)}, s32[8,64]{1,0:T(8,128)}, u32[]{:S(2)}) copy-start(s32[8,64]{1,0:T(8,128)} %param.17) | copy-start | bytes 6148
  32.1 2.6 %copy-start.7 = (s32[8]{0:T(128)S(1)}, s32[8]{0:T(128)}, u32[]{:S(2)}) copy-start(s32[8]{0:T(128)} %param.15) | copy-start | bytes 100
  36.5 18.3 %copy-start.9 = (f32[2048]{0:T(1024)S(1)}, f32[2048]{0:T(1024)}, u32[]{:S(2)}) copy-start(f32[2048]{0:T(1024)} %param.10) | copy-start | bytes 24580
  60.6 1.5 copy-start.2
  79.2 91.2 %copy-start.8 = (s32[8]{0:T(128)S(1)}, s32[8]{0:T(128)}, u32[]{:S(2)}) copy-start(s32[8]{0:T(128)} %param.16) | copy-start | bytes 100
  79.5 92.5 %copy-start.5 = (s32[8,64,1]{2,1,0:T(8,128)S(1)}, s32[8,64,1]{2,1,0:T(8,128)}, u32[]{:S(2)}) copy-start(s32[8,64,1]{2,1,0:T(8,128)} %add_maximum_fusion) | copy-start | bytes 6148
  79.8 92.3 %copy-start.6 = (bf16[8,2,64,128]{3,2,1,0:T(8,128)(2,1)}, bf16[8,2,64,128]{3,2,1,0:T(8,128)(2,1)S(1)}, u32[]{:S(2)}) copy-start(bf16[8,2,64,128]{3,2,1,0:T(8,128)(2,1)S(1)} %maximum_bitcast_fusion.3) | copy-start | bytes 786436
  165.3 52.7 %all-to-all-start.1 = ((bf16[16,1,2,256,128]{4,3,2,1,0:T(8,128)(2,1)}), bf16[16,1,2,256,128]{4,3,2,1,0:T(8,128)(2,1)S(1)}, u32[]{:S(2)}, u32[]{:S(2)}) async-start(bf16[16,1,2,256,128]{4,3,2,1,0:T(8,128)(2,1)} %constant_dynamic-slice_fusion.2), calls=%async_computation.1 | async-start | bytes 4194304 | tf_op jit(solution)/shard_map/all_to_all | solution.py:185
  172.1 30.7 %copy-start = (bf16[1024,2048]{1,0:T(8,128)(2,1)S(1)}, bf16[1024,2048]{1,0:T(8,128)(2,1)}, u32[]{:S(2)}) copy-start(bf16[1024,2048]{1,0:T(8,128)(2,1)} %param.13) | copy-start | bytes 12582916
  204.6 4.3 %copy-start.3 = (f32[6,64,2048]{2,1,0:T(8,128)}, f32[6,64,2048]{2,1,0:T(8,128)S(1)}, u32[]{:S(2)}) copy-start(f32[6,64,2048]{2,1,0:T(8,128)S(1)} %fusion.9) | copy-start | bytes 9437188
  205.7 24.0 %collective-permute-start.1 = (bf16[6,32,2048]{2,1,0:T(8,128)(2,1)}, bf16[6,32,2048]{2,1,0:T(8,128)(2,1)}, u32[]{:S(2)}, u32[]{:S(2)}) collective-permute-start(bf16[6,32,2048]{2,1,0:T(8,128)(2,1)} %slice.166), channel_id=1, source_target_pairs={{0,1},{1,0},{2,3},{3,2},{4,5},{5,4},{6,7},{7,6},{8,9},{9,8},{10,11... | collective-permute-start | bytes 2359304 | tf_op jit(solution)/shard_map/ppermute | solution.py:263
  218.1 9.6 %copy-start.1 = (bf16[1024,2048]{1,0:T(8,128)(2,1)S(1)}, bf16[1024,2048]{1,0:T(8,128)(2,1)}, u32[]{:S(2)}) copy-start(bf16[1024,2048]{1,0:T(8,128)(2,1)} %param.13) | copy-start | bytes 12582916
  227.6 2.1 copy-start.4
  228.4 8.1 %collective-permute-start.2 = (bf16[2,32,2048]{2,1,0:T(8,128)(2,1)S(1)}, bf16[2,32,2048]{2,1,0:T(8,128)(2,1)S(1)}, u32[]{:S(2)}, u32[]{:S(2)}) collective-permute-start(bf16[2,32,2048]{2,1,0:T(8,128)(2,1)S(1)} %slice.167), channel_id=1, source_target_pairs={{0,1},{1,0},{2,3},{3,2},{4,5},{5,4},{6,7},{7,6},{8,9},{9,8},{10,11... | collective-permute-start | bytes 786440 | tf_op jit(solution)/shard_map/ppermute | solution.py:263
where the time goes:
time: 239 us; the launch traced here: 238 us
  waiting for transfers between devices  112 us (47%)
  local copies, waits for them, and re-layouts  48.1 us (20%)
  Pallas kernels  40.2 us (17%)
  starting transfers between devices  15.2 us (6%)
  other arithmetic  13 us (5%)
  matrix products  9.6 us (4%)
    all_to_all x2, waiting for transfers between devices, exchange(): return lax.all_to_all(pages, 'req', split_axis=0, concat_axis=0, tiled=True)  94.7 us
    pallas_call x2, Pallas kernels, attend(): pl.pallas_call(functools.partial(attend_kernel, page_count, owners, group...  40.2 us
    transpose x1, local copies, waits for them, and re-layouts, per_device(): by_head = kv_pool.transpose(0, 2, 1, 3)  15.1 us
    ppermute x1, waiting for transfers between devices, per_device(): inputs = jnp.concatenate([hidden, lax.ppermute(hidden, 'tp', swap)], axis=0)  11.6 us
    all_to_all x2, starting transfers between devices, exchange(): return lax.all_to_all(pages, 'req', split_axis=0, concat_axis=0, tiled=True)  11.5 us
    dynamic_slice x2, local copies, waits for them, and re-layouts, per_device(): lax.dynamic_slice(by_head, (0, start, kv_first, 0, 0), (owners, stop - st...  9.41 us
    dot_general x1, matrix products, per_device(): jnp.einsum('trd,de->tre', normed, w_both, preferred_element_type=jnp.floa...  5.76 us
    ppermute x2, waiting for transfers between devices, per_device(): other = lax.ppermute(term[:, half:].astype(jnp.bfloat16), 'tp', swap)  5.46 us
  transfers between devices with their start and end apart: 5, of which 4 were waited for; matrix products, arithmetic and copies ran while one was open for 19% of the time, Pallas kernels for 17%

commit v1 on v0

--- a/solution.py
+++ b/solution.py
@@ -113,7 +113,7 @@
     lax.fori_loop(0, q_ref.shape[2] // rows, part, 0)
 
 
-def attend(me, q, kv, draft_kv, first, tree_bias, page_count):
+def attend(me, q, kv, base, draft_kv, first, tree_bias, page_count):
     count, kv_count, rows, width = q.shape
     owners = kv.shape[0]
     draft_len = first.shape[1]
@@ -128,7 +128,7 @@
             pl.BlockSpec(memory_space=pltpu.SMEM),
             pl.BlockSpec((1, 1, rows, width), lambda r, c: (r, c, 0, 0)),
             pl.BlockSpec(
-                (owners, 1) + kv.shape[2:], lambda r, c: (0, r // chunk_req, 0, 0, 0)
+                (owners, 1) + kv.shape[2:], lambda r, c: (0, base + r // chunk_req, 0, 0, 0)
             ),
             pl.BlockSpec((1, 1, draft_len, width), lambda r, c: (r, c, 0, 0)),
             pl.BlockSpec((1, draft_len, 1), lambda r, c: (r, 0, 0)),
@@ -170,22 +170,22 @@
 
     by_head = kv_pool.transpose(0, 2, 1, 3)
     by_head = by_head.reshape((owners, capacity) + by_head.shape[1:])
-    cuts = [0, capacity - 1, capacity] if capacity > 1 else [0, capacity]
+    cuts = [0, capacity // 2, capacity] if capacity > 1 else [0, capacity]
     spans = list(zip(cuts[:-1], cuts[1:]))
-    outgoing = [
-        lax.dynamic_slice(
+
+    def outgoing(span, head):
+        start, stop = span
+        return lax.dynamic_slice(
             by_head,
-            (0, start, kv_first, 0, 0),
+            (0, start, head, 0, 0),
             (owners, stop - start, kv_count) + by_head.shape[3:],
         )
-        for start, stop in spans
-    ]
 
     def exchange(pages):
         return lax.all_to_all(pages, "req", split_axis=0, concat_axis=0, tiled=True)
 
-    first_out, hidden, w_keyval, parents, cache_len = lax.optimization_barrier(
-        (outgoing[0], hidden, w_keyval, parents, cache_len)
+    first_out, head_later, hidden, w_keyval, parents, cache_len = lax.optimization_barrier(
+        (outgoing(spans[0], kv_first), kv_first, hidden, w_keyval, parents, cache_len)
     )
     windows = [exchange(first_out)]
 
@@ -241,17 +241,24 @@
 
     if len(spans) > 1:
         last, windows[0], queries, draft_kv, first_slot, tree_bias = lax.optimization_barrier(
-            (outgoing[1], windows[0], queries, draft_kv, first_slot, tree_bias)
+            (outgoing(spans[1], head_later), windows[0], queries, draft_kv, first_slot, tree_bias)
         )
         windows.append(exchange(last))
 
     results = []
+    parts = []
     for window, (start, stop) in zip(windows, spans):
+        if start == 0:
+            parts.append((window, 0, start, stop))
+        else:
+            parts.extend((window, copy - start, copy, copy + 1) for copy in range(start, stop))
+    for window, base, start, stop in parts:
         here = slice(start * chunk_req, stop * chunk_req)
         mixed = attend(
             me,
             queries[here],
             window,
+            base,
             draft_kv[here],
             first_slot[here],
             tree_bias[here],

time: 239 us -> 252 us (1.054)
  waiting for transfers between devices: 112 us -> 126 us
  local copies, waits for them, and re-layouts: 48.1 us -> 43.1 us
  Pallas kernels: 40.2 us -> 43.6 us
    ppermute x2 -> x3, waiting for transfers between devices: 5.46 us -> 18.8 us  [per_device(): other = lax.ppermute(term[:, half:].astype(jnp.bfloat16), 'tp', swap)]
    pallas_call x2 -> x3, Pallas kernels: 40.2 us -> 43.6 us  [attend(): pl.pallas_call(functools.partial(attend_kernel, page_count, owners, group...]
    all_to_all x2, waiting for transfers between devices: 94.7 us -> 98 us  [exchange(): return lax.all_to_all(pages, 'req', split_axis=0, concat_axis=0, tiled=True)]
    ppermute x1, waiting for transfers between devices: 11.6 us -> 8.88 us  [per_device(): inputs = jnp.concatenate([hidden, lax.ppermute(hidden, 'tp', swap)], axis=0)]
  transfers between devices with their start and end apart: 5 -> 6, of which waited for: 4 -> 5; matrix products, arithmetic and copies ran while one was open for 19% -> 16% of each run, Pallas kernels for 17% -> 13%
where the time goes in v1:
time: 252 us; the launch traced here: 251 us
  waiting for transfers between devices  126 us (50%)
  Pallas kernels  43.6 us (17%)
  local copies, waits for them, and re-layouts  43.1 us (17%)
  starting transfers between devices  15.5 us (6%)
  other arithmetic  12.7 us (5%)
  matrix products  9.7 us (4%)
    all_to_all x2, waiting for transfers between devices, exchange(): return lax.all_to_all(pages, 'req', split_axis=0, concat_axis=0, tiled=True)  98 us
    pallas_call x3, Pallas kernels, attend(): pl.pallas_call(functools.partial(attend_kernel, page_count, owners, group...  43.6 us
    ppermute x3, waiting for transfers between devices, per_device(): other = lax.ppermute(term[:, half:].astype(jnp.bfloat16), 'tp', swap)  18.8 us
    transpose x1, local copies, waits for them, and re-layouts, per_device(): by_head = kv_pool.transpose(0, 2, 1, 3)  15.1 us
    all_to_all x2, starting transfers between devices, exchange(): return lax.all_to_all(pages, 'req', split_axis=0, concat_axis=0, tiled=True)  11.5 us
    dynamic_slice x2, local copies, waits for them, and re-layouts, outgoing(): lax.dynamic_slice(by_head, (0, start, head, 0, 0), (owners, stop - start,...  9.33 us
    ppermute x1, waiting for transfers between devices, per_device(): inputs = jnp.concatenate([hidden, lax.ppermute(hidden, 'tp', swap)], axis=0)  8.88 us
    dot_general x1, matrix products, per_device(): jnp.einsum('trd,de->tre', normed, w_both, preferred_element_type=jnp.floa...  5.76 us
  transfers between devices with their start and end apart: 6, of which 5 were waited for; matrix products, arithmetic and copies ran while one was open for 16% of the time, Pallas kernels for 13%

profile of v1, /device:TPU:13, one launch (start us, length us, event | category | flops | bytes accessed | tf_op | source)
XLA Modules:
  0.0 250.8 jit_solution(714575561507169630)
XLA Ops:
  0.0 15.1 %copy.97 = bf16[64,4,256,128]{3,2,1,0:T(8,128)(2,1)} copy(bf16[64,4,256,128]{3,1,2,0:T(4,128)(2,1)} %bitcast.55) | data formatting | bytes 33554432 | tf_op jit(solution)/shard_map/transpose | solution.py:171
  15.1 4.7 %constant_dynamic-slice_fusion.2 = bf16[16,2,2,256,128]{4,3,2,1,0:T(8,128)(2,1)} fusion(bf16[16,4,4,256,128]{4,3,2,1,0:T(8,128)(2,1)} %bitcast.53, s32[]{:T(128)S(6)} %select_n.73), kind=kLoop, calls=%fused_computation.112 | loop fusion | bytes 8388612 | tf_op jit(solution)/shard_map/dynamic_slice | solution.py:178
  19.8 6.6 %all-to-all-start = ((bf16[16,2,2,256,128]{4,3,2,1,0:T(8,128)(2,1)}), bf16[16,2,2,256,128]{4,3,2,1,0:T(8,128)(2,1)}, u32[]{:S(2)}, u32[]{:S(2)}) async-start(bf16[16,2,2,256,128]{4,3,2,1,0:T(8,128)(2,1)} %constant_dynamic-slice_fusion.2), calls=%async_computation | async-start | bytes 8388608 | tf_op jit(solution)/shard_map/all_to_all | solution.py:185
  26.3 1.2 collective-permute-start
  27.5 3.0 %copy.100 = bf16[2048,4,128]{0,2,1:T(8,128)(2,1)S(1)} copy(bf16[2048,4,128]{2,1,0:T(4,128)(2,1)} %param.12) | data formatting | bytes 4194304 | tf_op jit(solution)/shard_map/optimization_barrier | solution.py:187
  30.5 0.1 constant_dynamic-slice_fusion
  30.7 0.5 copy.101
  31.2 0.3 fusion.39
  31.6 0.2 fusion.38
  31.9 0.2 fusion.37
  32.2 0.2 fusion.36
  32.4 0.2 fusion.35
  32.7 0.2 fusion.34
  32.9 0.1 convert_reduce_fusion
  33.2 1.0 multiply_cosine_fusion
  34.2 0.2 copy.105
  34.4 0.5 copy-done.3
  34.9 0.2 copy.104
  35.1 0.1 copy.111
  35.3 0.2 copy.112
  35.6 4.7 %constant_dynamic-slice_fusion.1 = bf16[16,2,2,256,128]{4,3,2,1,0:T(8,128)(2,1)} fusion(bf16[16,4,4,256,128]{4,3,2,1,0:T(8,128)(2,1)} %bitcast.54, s32[]{:T(128)S(6)} %select_n.74), kind=kLoop, calls=%fused_computation.111 | loop fusion | bytes 8388612 | tf_op jit(solution)/shard_map/dynamic_slice | solution.py:178
  40.3 0.1 add_select_fusion
  40.4 0.1 fusion.74
  40.5 0.8 fusion.60
  41.3 0.8 add_maximum_fusion
  42.2 8.9 %collective-permute-done = bf16[32,8,2048]{2,1,0:T(8,128)(2,1)} collective-permute-done((bf16[32,8,2048]{2,1,0:T(8,128)(2,1)}, bf16[32,8,2048]{2,1,0:T(8,128)(2,1)}, u32[]{:S(2)}, u32[]{:S(2)}) %collective-permute-start) | collective-permute-done | bytes 1048608 | tf_op jit(solution)/shard_map/ppermute | solution.py:197
  51.0 2.0 fusion.3
  53.1 0.1 copy.99
  53.2 5.8 %fusion = f32[64,8,1280]{2,1,0:T(8,128)S(1)} fusion(bf16[2048,256]{1,0:T(8,128)(2,1)S(1)} %copy.101, bf16[2048,1024]{1,0:T(8,128)(2,1)} %param.11, f32[2048]{0:T(1024)S(1)} %copy-done.11, f32[64,8]{1,0:T(8,128)S(1)} %copy.99, bf16[32,8,2048]{2,1,0:T(8,128)(2,1)} %collective-permute-done, bf16[32,8,2048]{2,1,0:T(8,128)(2,1)} %param.9), kind=kOutput, calls=%fused_computation.3 | convolution fusion | flops 2700083200 | bytes 9971712 | tf_op jit(solution)/shard_map/trd,de->tre/dot_general | solution.py:210
  59.0 1.5 copy-done.2
  60.5 0.3 slice.159
  60.8 2.5 %reshape.154 = f32[64,8,16,64]{3,2,1,0:T(8,128)} reshape(f32[64,8,1024]{2,1,0:T(8,128)S(1)} %slice.159) | data formatting | bytes 4194304 | tf_op jit(solution)/shard_map/reshape | solution.py:222
  63.4 4.7 %multiply_subtract_fusion = (f32[64,8,16,32]{3,2,1,0:T(8,128)S(1)}, f32[64,8,16,32]{3,2,1,0:T(8,128)S(1)}) fusion(f32[64,8,16,64]{3,2,1,0:T(8,128)} %reshape.154, f32[64,8,32]{2,1,0:T(8,128)S(1)} %copy.105, f32[64,8,32]{2,1,0:T(8,128)S(1)} %copy.104), kind=kLoop, calls=%fused_computation.18 | loop fusion | flops 1572864 | bytes 4325376 | tf_op jit(solution)/shard_map/sub | solution.py:43
  68.1 2.4 copy.107
  70.5 2.4 copy.106
  73.0 1.1 slice_bitcast_fusion
  74.0 0.1 slice.165
  74.3 1.2 fusion.6
  75.5 0.5 pad.4
  76.0 0.2 fusion.70
  76.2 0.2 copy-done.4
  76.4 0.1 copy-done.6
  76.5 0.4 subtract_convert_fusion
  76.8 0.3 maximum_bitcast_fusion.3
  77.1 41.7 %all-to-all-done.kv_ref = bf16[16,2,2,256,128]{4,3,2,1,0:T(8,128)(2,1)} async-done(((bf16[16,2,2,256,128]{4,3,2,1,0:T(8,128)(2,1)}), bf16[16,2,2,256,128]{4,3,2,1,0:T(8,128)(2,1)}, u32[]{:S(2)}, u32[]{:S(2)}) %all-to-all-start) | async-done | bytes 4194336 | tf_op jit(solution)/shard_map/all_to_all | solution.py:185
  118.8 4.9 %all-to-all-start.1 = ((bf16[16,2,2,256,128]{4,3,2,1,0:T(8,128)(2,1)}), bf16[16,2,2,256,128]{4,3,2,1,0:T(8,128)(2,1)}, u32[]{:S(2)}, u32[]{:S(2)}) async-start(bf16[16,2,2,256,128]{4,3,2,1,0:T(8,128)(2,1)} %constant_dynamic-slice_fusion.1), calls=%async_computation.1 | async-start | bytes 8388608 | tf_op jit(solution)/shard_map/all_to_all | solution.py:185
  123.8 0.1 broadcast_select_fusion
  124.1 21.0 %shard_map.91 = bf16[4,64,1024]{2,1,0:T(8,128)(2,1)S(1)} custom-call(s32[1]{0:T(128)} %bitcast.1.me_ref, bf16[4,2,512,128]{3,2,1,0:T(8,128)(2,1)S(1)} %slice.139.q_ref, bf16[16,2,2,256,128]{4,3,2,1,0:T(8,128)(2,1)} %all-to-all-done.kv_ref, bf16[4,2,64,128]{3,2,1,0:T(8,128)(2,1)S(1)} %slice.140.dkv_ref, s32[4,64,1]{2,1,0:T(8,128)S(1)} %slice.141.first_ref, ...), custom_call_target="tpu_custom_call" | custom-call | flops 4429185024 | bytes 6291456 | tf_op jit(solution)/shard_map/pallas_call | solution.py:124
  145.2 1.2 fusion.11
  146.5 1.3 collective-permute-start.1
  147.9 11.8 %collective-permute-done.1 = bf16[4,32,2048]{2,1,0:T(8,128)(2,1)S(1)} collective-permute-done((bf16[4,32,2048]{2,1,0:T(8,128)(2,1)S(1)}, bf16[4,32,2048]{2,1,0:T(8,128)(2,1)S(1)}, u32[]{:S(2)}, u32[]{:S(2)}) %collective-permute-start.1) | collective-permute-done | bytes 524320 | tf_op jit(solution)/shard_map/ppermute | solution.py:270
  159.7 0.2 fusion.41
  159.9 56.3 %all-to-all-done.1.kv_ref = bf16[16,2,2,256,128]{4,3,2,1,0:T(8,128)(2,1)} async-done(((bf16[16,2,2,256,128]{4,3,2,1,0:T(8,128)(2,1)}), bf16[16,2,2,256,128]{4,3,2,1,0:T(8,128)(2,1)}, u32[]{:S(2)}, u32[]{:S(2)}) %all-to-all-start.1) | async-done | bytes 4194336 | tf_op jit(solution)/shard_map/all_to_all | solution.py:185
  216.2 11.4 %shard_map.93 = bf16[2,64,1024]{2,1,0:T(8,128)(2,1)S(1)} custom-call(s32[1]{0:T(128)} %bitcast.1.me_ref, bf16[2,2,512,128]{3,2,1,0:T(8,128)(2,1)S(1)} %get-tuple-element.32.q_ref, bf16[16,2,2,256,128]{4,3,2,1,0:T(8,128)(2,1)} %all-to-all-done.1.kv_ref, bf16[2,2,64,128]{3,2,1,0:T(8,128)(2,1)S(1)} %get-tuple-element.42.dkv_ref, ...), custom_call_target="tpu_custom_call" | custom-call | flops 2214592512 | bytes 5242880 | tf_op jit(solution)/shard_map/pallas_call | solution.py:124
  227.6 0.7 fusion.7
  228.3 1.3 collective-permute-start.3
  229.6 11.2 %shard_map.92 = bf16[2,64,1024]{2,1,0:T(8,128)(2,1)S(1)} custom-call(s32[1]{0:T(128)} %bitcast.1.me_ref, bf16[2,2,512,128]{3,2,1,0:T(8,128)(2,1)S(1)} %get-tuple-element.31.q_ref, bf16[16,2,2,256,128]{4,3,2,1,0:T(8,128)(2,1)} %all-to-all-done.1.kv_ref, bf16[2,2,64,128]{3,2,1,0:T(8,128)(2,1)S(1)} %get-tuple-element.41.dkv_ref, ...), custom_call_target="tpu_custom_call" | custom-call | flops 2214592512 | bytes 5242880 | tf_op jit(solution)/shard_map/pallas_call | solution.py:124
  240.8 0.7 fusion.9
  241.6 0.3 collective-permute-start.2
  241.9 0.1 fusion.43
  242.0 7.0 %collective-permute-done.2 = bf16[2,32,2048]{2,1,0:T(8,128)(2,1)S(1)} collective-permute-done((bf16[2,32,2048]{2,1,0:T(8,128)(2,1)S(1)}, bf16[2,32,2048]{2,1,0:T(8,128)(2,1)S(1)}, u32[]{:S(2)}, u32[]{:S(2)}) %collective-permute-start.2) | collective-permute-done | bytes 262176 | tf_op jit(solution)/shard_map/ppermute | solution.py:270
  249.0 0.1 fusion.45
  249.1 0.1 maximum_bitcast_fusion.2
  249.2 1.5 copy.113
  (58 shorter events, 1.3 us)
Async XLA Ops:
  19.8 99.0 %all-to-all-start = ((bf16[16,2,2,256,128]{4,3,2,1,0:T(8,128)(2,1)}), bf16[16,2,2,256,128]{4,3,2,1,0:T(8,128)(2,1)}, u32[]{:S(2)}, u32[]{:S(2)}) async-start(bf16[16,2,2,256,128]{4,3,2,1,0:T(8,128)(2,1)} %constant_dynamic-slice_fusion.2), calls=%async_computation | async-start | bytes 8388608 | tf_op jit(solution)/shard_map/all_to_all | solution.py:185
  26.3 24.7 %collective-permute-start = (bf16[32,8,2048]{2,1,0:T(8,128)(2,1)}, bf16[32,8,2048]{2,1,0:T(8,128)(2,1)}, u32[]{:S(2)}, u32[]{:S(2)}) collective-permute-start(bf16[32,8,2048]{2,1,0:T(8,128)(2,1)} %param.9), channel_id=1, source_target_pairs={{0,1},{1,0},{2,3},{3,2},{4,5},{5,4},{6,7},{7,6},{8,9},{9,8},{10,11... | collective-permute-start | bytes 3145736 | tf_op jit(solution)/shard_map/ppermute | solution.py:197
  27.5 3.7 %copy-start.12 = (s32[8,64]{1,0:T(8,128)S(1)}, s32[8,64]{1,0:T(8,128)}, u32[]{:S(2)}) copy-start(s32[8,64]{1,0:T(8,128)} %param.17) | copy-start | bytes 6148
  30.5 2.6 %copy-start.9 = (s32[8]{0:T(128)S(1)}, s32[8]{0:T(128)}, u32[]{:S(2)}) copy-start(s32[8]{0:T(128)} %param.15) | copy-start | bytes 100
  34.2 0.7 copy-start.3
  34.2 0.9 copy-start.5
  35.6 17.6 %copy-start.11 = (f32[2048]{0:T(1024)S(1)}, f32[2048]{0:T(1024)}, u32[]{:S(2)}) copy-start(f32[2048]{0:T(1024)} %param.10) | copy-start | bytes 24580
  59.0 1.5 copy-start.2
  75.5 1.0 copy-start.4
  75.5 1.0 copy-start.6
  77.1 46.8 %copy-start.10 = (s32[8]{0:T(128)S(1)}, s32[8]{0:T(128)}, u32[]{:S(2)}) copy-start(s32[8]{0:T(128)} %param.16) | copy-start | bytes 100
  77.1 46.9 %copy-start.8 = (s32[8,64,1]{2,1,0:T(8,128)S(1)}, s32[8,64,1]{2,1,0:T(8,128)}, u32[]{:S(2)}) copy-start(s32[8,64,1]{2,1,0:T(8,128)} %add_maximum_fusion) | copy-start | bytes 6148
  77.1 47.0 %copy-start.7 = (f32[8,64,64]{2,1,0:T(8,128)S(1)}, f32[8,64,64]{2,1,0:T(8,128)}, u32[]{:S(2)}) copy-start(f32[8,64,64]{2,1,0:T(8,128)} %fusion.60) | copy-start | bytes 393220
  118.8 97.4 %all-to-all-start.1 = ((bf16[16,2,2,256,128]{4,3,2,1,0:T(8,128)(2,1)}), bf16[16,2,2,256,128]{4,3,2,1,0:T(8,128)(2,1)}, u32[]{:S(2)}, u32[]{:S(2)}) async-start(bf16[16,2,2,256,128]{4,3,2,1,0:T(8,128)(2,1)} %constant_dynamic-slice_fusion.1), calls=%async_computation.1 | async-start | bytes 8388608 | tf_op jit(solution)/shard_map/all_to_all | solution.py:185
  124.1 21.0 %copy-start = (bf16[1024,2048]{1,0:T(8,128)(2,1)S(1)}, bf16[1024,2048]{1,0:T(8,128)(2,1)}, u32[]{:S(2)}) copy-start(bf16[1024,2048]{1,0:T(8,128)(2,1)} %param.13) | copy-start | bytes 12582916
  146.5 13.2 %collective-permute-start.1 = (bf16[4,32,2048]{2,1,0:T(8,128)(2,1)S(1)}, bf16[4,32,2048]{2,1,0:T(8,128)(2,1)S(1)}, u32[]{:S(2)}, u32[]{:S(2)}) collective-permute-start(bf16[4,32,2048]{2,1,0:T(8,128)(2,1)S(1)} %slice.204), channel_id=1, source_target_pairs={{0,1},{1,0},{2,3},{3,2},{4,5},{5,4},{6,7},{7,6},{8,9},{9,8},{10,11... | collective-permute-start | bytes 1572872 | tf_op jit(solution)/shard_map/ppermute | solution.py:270
  216.2 11.4 %copy-start.1 = (bf16[1024,2048]{1,0:T(8,128)(2,1)S(1)}, bf16[1024,2048]{1,0:T(8,128)(2,1)}, u32[]{:S(2)}) copy-start(bf16[1024,2048]{1,0:T(8,128)(2,1)} %param.13) | copy-start | bytes 12582916
  228.3 13.6 %collective-permute-start.3 = (bf16[2,32,2048]{2,1,0:T(8,128)(2,1)S(1)}, bf16[2,32,2048]{2,1,0:T(8,128)(2,1)S(1)}, u32[]{:S(2)}, u32[]{:S(2)}) collective-permute-start(bf16[2,32,2048]{2,1,0:T(8,128)(2,1)S(1)} %slice.205), channel_id=1, source_target_pairs={{0,1},{1,0},{2,3},{3,2},{4,5},{5,4},{6,7},{7,6},{8,9},{9,8},{10,11... | collective-permute-start | bytes 786440 | tf_op jit(solution)/shard_map/ppermute | solution.py:270
  241.6 7.4 %collective-permute-start.2 = (bf16[2,32,2048]{2,1,0:T(8,128)(2,1)S(1)}, bf16[2,32,2048]{2,1,0:T(8,128)(2,1)S(1)}, u32[]{:S(2)}, u32[]{:S(2)}) collective-permute-start(bf16[2,32,2048]{2,1,0:T(8,128)(2,1)S(1)} %slice.206), channel_id=1, source_target_pairs={{0,1},{1,0},{2,3},{3,2},{4,5},{5,4},{6,7},{7,6},{8,9},{9,8},{10,11... | collective-permute-start | bytes 786440 | tf_op jit(solution)/shard_map/ppermute | solution.py:270

commit v2 on v0

--- a/solution.py
+++ b/solution.py
@@ -120,7 +120,7 @@
     slots = page_count * kv.shape[3] + draft_len
     chunk_req = owners // page_count
     columns = rows // draft_len * (width // 2)
-    groups_at_once = math.gcd(rows // draft_len, 4)
+    groups_at_once = math.gcd(rows // draft_len, 8)
     return pl.pallas_call(
         functools.partial(attend_kernel, page_count, owners, groups_at_once),
         grid=(count, kv_count),

time: 239 us -> 240 us (level)
  Pallas kernels: 40.2 us -> 44.8 us
  waiting for transfers between devices: 112 us -> 108 us
    pallas_call x2, Pallas kernels: 40.2 us -> 44.8 us  [attend(): pl.pallas_call(functools.partial(attend_kernel, page_count, owners, group...]
    all_to_all x2, waiting for transfers between devices: 94.7 us -> 91.2 us  [exchange(): return lax.all_to_all(pages, 'req', split_axis=0, concat_axis=0, tiled=True)]
  transfers between devices with their start and end apart: 5 -> 5, of which waited for: 4 -> 4; matrix products, arithmetic and copies ran while one was open for 19% -> 19% of each run, Pallas kernels for 17% -> 19%
where the time goes in v2:
time: 240 us; the launch traced here: 239 us
  waiting for transfers between devices  108 us (45%)
  local copies, waits for them, and re-layouts  48.1 us (20%)
  Pallas kernels  44.8 us (19%)
  starting transfers between devices  15.2 us (6%)
  other arithmetic  13 us (5%)
  matrix products  9.6 us (4%)
    all_to_all x2, waiting for transfers between devices, exchange(): return lax.all_to_all(pages, 'req', split_axis=0, concat_axis=0, tiled=True)  91.2 us
    pallas_call x2, Pallas kernels, attend(): pl.pallas_call(functools.partial(attend_kernel, page_count, owners, group...  44.8 us
    transpose x1, local copies, waits for them, and re-layouts, per_device(): by_head = kv_pool.transpose(0, 2, 1, 3)  15.1 us
    ppermute x1, waiting for transfers between devices, per_device(): inputs = jnp.concatenate([hidden, lax.ppermute(hidden, 'tp', swap)], axis=0)  11.6 us
    all_to_all x2, starting transfers between devices, exchange(): return lax.all_to_all(pages, 'req', split_axis=0, concat_axis=0, tiled=True)  11.5 us
    dynamic_slice x2, local copies, waits for them, and re-layouts, per_device(): lax.dynamic_slice(by_head, (0, start, kv_first, 0, 0), (owners, stop - st...  9.41 us
    dot_general x1, matrix products, per_device(): jnp.einsum('trd,de->tre', normed, w_both, preferred_element_type=jnp.floa...  5.76 us
    ppermute x2, waiting for transfers between devices, per_device(): other = lax.ppermute(term[:, half:].astype(jnp.bfloat16), 'tp', swap)  5.46 us
  transfers between devices with their start and end apart: 5, of which 4 were waited for; matrix products, arithmetic and copies ran while one was open for 19% of the time, Pallas kernels for 19%

profile of v2, /device:TPU:13, one launch (start us, length us, event | category | flops | bytes accessed | tf_op | source)
XLA Modules:
  0.0 239.4 jit_solution(15484742788921974440)
XLA Ops:
  0.0 15.1 %copy.97 = bf16[64,4,256,128]{3,2,1,0:T(8,128)(2,1)} copy(bf16[64,4,256,128]{3,1,2,0:T(4,128)(2,1)} %bitcast.50) | data formatting | bytes 33554432 | tf_op jit(solution)/shard_map/transpose | solution.py:171
  15.1 6.2 %constant_dynamic-slice_fusion.1 = bf16[16,3,2,256,128]{4,3,2,1,0:T(8,128)(2,1)} fusion(bf16[16,4,4,256,128]{4,3,2,1,0:T(8,128)(2,1)} %bitcast.48, s32[]{:T(128)S(6)} %select_n.68), kind=kLoop, calls=%fused_computation.104 | loop fusion | bytes 12582916 | tf_op jit(solution)/shard_map/dynamic_slice | solution.py:176
  21.4 6.6 %all-to-all-start = ((bf16[16,3,2,256,128]{4,3,2,1,0:T(8,128)(2,1)}), bf16[16,3,2,256,128]{4,3,2,1,0:T(8,128)(2,1)}, u32[]{:S(2)}, u32[]{:S(2)}) async-start(bf16[16,3,2,256,128]{4,3,2,1,0:T(8,128)(2,1)} %constant_dynamic-slice_fusion.1), calls=%async_computation | async-start | bytes 12582912 | tf_op jit(solution)/shard_map/all_to_all | solution.py:185
  27.9 1.2 collective-permute-start
  29.1 3.0 %copy.100 = bf16[2048,4,128]{0,2,1:T(8,128)(2,1)S(1)} copy(bf16[2048,4,128]{2,1,0:T(4,128)(2,1)} %param.12) | data formatting | bytes 4194304 | tf_op jit(solution)/shard_map/optimization_barrier | solution.py:187
  32.1 0.1 constant_dynamic-slice_fusion
  32.3 0.5 copy.101
  32.8 0.3 fusion.39
  33.2 0.2 fusion.38
  33.5 0.2 fusion.37
  33.8 0.2 fusion.36
  34.0 0.2 fusion.35
  34.3 0.2 fusion.34
  34.5 0.1 convert_reduce_fusion
  34.7 0.1 slice_bitcast_fusion.4
  34.7 0.1 fusion.62
  34.8 1.0 multiply_cosine_fusion
  35.8 0.2 copy.105
  36.0 0.2 copy.104
  36.1 0.1 copy.111
  36.3 0.1 pad_add_fusion
  36.4 0.2 copy.112
  36.5 0.1 convert_compare_fusion
  36.6 3.2 %constant_dynamic-slice_fusion.2 = bf16[16,1,2,256,128]{4,3,2,1,0:T(8,128)(2,1)} fusion(bf16[16,4,4,256,128]{4,3,2,1,0:T(8,128)(2,1)} %bitcast.49, s32[]{:T(128)S(6)} %select_n.68), kind=kLoop, calls=%fused_computation.105 | loop fusion | bytes 4194308 | tf_op jit(solution)/shard_map/dynamic_slice | solution.py:176
  39.8 0.1 add_select_fusion
  39.9 0.1 fusion.66
  40.1 0.1 fusion.56
  40.2 0.8 add_maximum_fusion
  41.0 11.6 %collective-permute-done = bf16[32,8,2048]{2,1,0:T(8,128)(2,1)} collective-permute-done((bf16[32,8,2048]{2,1,0:T(8,128)(2,1)}, bf16[32,8,2048]{2,1,0:T(8,128)(2,1)}, u32[]{:S(2)}, u32[]{:S(2)}) %collective-permute-start) | collective-permute-done | bytes 1048608 | tf_op jit(solution)/shard_map/ppermute | solution.py:197
  52.6 2.0 fusion.3
  54.7 0.1 copy.99
  54.8 5.8 %fusion = f32[64,8,1280]{2,1,0:T(8,128)S(1)} fusion(bf16[2048,256]{1,0:T(8,128)(2,1)S(1)} %copy.101, bf16[2048,1024]{1,0:T(8,128)(2,1)} %param.11, f32[2048]{0:T(1024)S(1)} %copy-done.9, f32[64,8]{1,0:T(8,128)S(1)} %copy.99, bf16[32,8,2048]{2,1,0:T(8,128)(2,1)} %collective-permute-done, bf16[32,8,2048]{2,1,0:T(8,128)(2,1)} %param.9), kind=kOutput, calls=%fused_computation.3 | convolution fusion | flops 2700083200 | bytes 9971712 | tf_op jit(solution)/shard_map/trd,de->tre/dot_general | solution.py:210
  60.6 1.5 copy-done.2
  62.1 0.3 slice.130
  62.4 2.5 %reshape.153 = f32[64,8,16,64]{3,2,1,0:T(8,128)} reshape(f32[64,8,1024]{2,1,0:T(8,128)S(1)} %slice.130) | data formatting | bytes 4194304 | tf_op jit(solution)/shard_map/reshape | solution.py:222
  64.9 4.7 %multiply_subtract_fusion = (f32[64,8,16,32]{3,2,1,0:T(8,128)S(1)}, f32[64,8,16,32]{3,2,1,0:T(8,128)S(1)}) fusion(f32[64,8,16,64]{3,2,1,0:T(8,128)} %reshape.153, f32[64,8,32]{2,1,0:T(8,128)S(1)} %copy.105, f32[64,8,32]{2,1,0:T(8,128)S(1)} %copy.104), kind=kLoop, calls=%fused_computation.16 | loop fusion | flops 1572864 | bytes 4325376 | tf_op jit(solution)/shard_map/sub | solution.py:43
  69.7 2.4 %copy.107 = f32[64,8,16,32]{3,0,2,1:T(8,128)S(1)} copy(f32[64,8,16,32]{3,2,1,0:T(8,128)S(1)} %get-tuple-element.28) | data formatting | bytes 2097152 | tf_op jit(solution)/shard_map/add | solution.py:44
  72.1 2.4 %copy.106 = f32[64,8,16,32]{3,0,2,1:T(8,128)S(1)} copy(f32[64,8,16,32]{3,2,1,0:T(8,128)S(1)} %get-tuple-element.27) | data formatting | bytes 2097152 | tf_op jit(solution)/shard_map/sub | solution.py:43
  74.6 1.1 slice_bitcast_fusion
  75.6 0.1 slice.136
  75.9 1.2 fusion.6
  77.0 1.9 pad.4
  79.0 0.2 fusion.65
  79.2 0.4 subtract_convert_fusion
  79.6 0.3 maximum_bitcast_fusion.3
  79.8 85.5 %all-to-all-done.kv_ref = bf16[16,3,2,256,128]{4,3,2,1,0:T(8,128)(2,1)} async-done(((bf16[16,3,2,256,128]{4,3,2,1,0:T(8,128)(2,1)}), bf16[16,3,2,256,128]{4,3,2,1,0:T(8,128)(2,1)}, u32[]{:S(2)}, u32[]{:S(2)}) %all-to-all-start) | async-done | bytes 6291488 | tf_op jit(solution)/shard_map/all_to_all | solution.py:185
  165.3 4.9 %all-to-all-start.1 = ((bf16[16,1,2,256,128]{4,3,2,1,0:T(8,128)(2,1)}), bf16[16,1,2,256,128]{4,3,2,1,0:T(8,128)(2,1)S(1)}, u32[]{:S(2)}, u32[]{:S(2)}) async-start(bf16[16,1,2,256,128]{4,3,2,1,0:T(8,128)(2,1)} %constant_dynamic-slice_fusion.2), calls=%async_computation.1 | async-start | bytes 4194304 | tf_op jit(solution)/shard_map/all_to_all | solution.py:185
  170.3 0.1 broadcast_select_fusion
  170.5 1.5 slice.117.q_ref
  172.1 34.1 %shard_map.91 = bf16[6,64,1024]{2,1,0:T(8,128)(2,1)S(1)} custom-call(s32[1]{0:T(128)} %bitcast.1.me_ref, bf16[6,2,512,128]{3,2,1,0:T(8,128)(2,1)S(1)} %slice.117.q_ref, bf16[16,3,2,256,128]{4,3,2,1,0:T(8,128)(2,1)} %all-to-all-done.kv_ref, bf16[6,2,64,128]{3,2,1,0:T(8,128)(2,1)S(1)} %slice.118.dkv_ref, s32[6,64,1]{2,1,0:T(8,128)S(1)} %slice.119.first_ref, ...), custom_call_target="tpu_custom_call" | custom-call | flops 6643777536 | bytes 9437184 | tf_op jit(solution)/shard_map/pallas_call | solution.py:124
  206.2 1.8 fusion.9
  208.1 1.1 slice.166
  209.2 1.2 collective-permute-start.1
  210.4 1.1 slice.124.q_ref
  211.5 0.8 slice.125.dkv_ref
  212.4 5.7 %all-to-all-done.1.kv_ref = bf16[16,1,2,256,128]{4,3,2,1,0:T(8,128)(2,1)S(1)} async-done(((bf16[16,1,2,256,128]{4,3,2,1,0:T(8,128)(2,1)}), bf16[16,1,2,256,128]{4,3,2,1,0:T(8,128)(2,1)S(1)}, u32[]{:S(2)}, u32[]{:S(2)}) %all-to-all-start.1) | async-done | bytes 2097184 | tf_op jit(solution)/shard_map/all_to_all | solution.py:185
  218.1 10.7 %shard_map.92 = bf16[2,64,1024]{2,1,0:T(8,128)(2,1)S(1)} custom-call(s32[1]{0:T(128)} %bitcast.1.me_ref, bf16[2,2,512,128]{3,2,1,0:T(8,128)(2,1)S(1)} %slice.124.q_ref, bf16[16,1,2,256,128]{4,3,2,1,0:T(8,128)(2,1)S(1)} %all-to-all-done.1.kv_ref, bf16[2,2,64,128]{3,2,1,0:T(8,128)(2,1)S(1)} %slice.125.dkv_ref, s32[2,64,1]{2,1,0:T(8,128)S(1)} %slice.126.first_ref, ...), custom_call_target="tpu_custom_call" | custom-call | flops 2214592512 | bytes 3145728 | tf_op jit(solution)/shard_map/pallas_call | solution.py:124
  228.8 0.7 fusion.7
  229.6 1.3 collective-permute-start.2
  230.9 1.4 fusion.15
  232.2 5.5 %collective-permute-done.2 = bf16[2,32,2048]{2,1,0:T(8,128)(2,1)S(1)} collective-permute-done((bf16[2,32,2048]{2,1,0:T(8,128)(2,1)S(1)}, bf16[2,32,2048]{2,1,0:T(8,128)(2,1)S(1)}, u32[]{:S(2)}, u32[]{:S(2)}) %collective-permute-start.2) | collective-permute-done | bytes 262176 | tf_op jit(solution)/shard_map/ppermute | solution.py:263
  237.7 0.1 fusion.41
  237.8 0.1 maximum_bitcast_fusion.2
  237.9 1.5 copy.113
  (48 shorter events, 0.8 us)
Async XLA Ops:
  21.4 144.0 %all-to-all-start = ((bf16[16,3,2,256,128]{4,3,2,1,0:T(8,128)(2,1)}), bf16[16,3,2,256,128]{4,3,2,1,0:T(8,128)(2,1)}, u32[]{:S(2)}, u32[]{:S(2)}) async-start(bf16[16,3,2,256,128]{4,3,2,1,0:T(8,128)(2,1)} %constant_dynamic-slice_fusion.1), calls=%async_computation | async-start | bytes 12582912 | tf_op jit(solution)/shard_map/all_to_all | solution.py:185
  27.9 24.7 %collective-permute-start = (bf16[32,8,2048]{2,1,0:T(8,128)(2,1)}, bf16[32,8,2048]{2,1,0:T(8,128)(2,1)}, u32[]{:S(2)}, u32[]{:S(2)}) collective-permute-start(bf16[32,8,2048]{2,1,0:T(8,128)(2,1)} %param.9), channel_id=1, source_target_pairs={{0,1},{1,0},{2,3},{3,2},{4,5},{5,4},{6,7},{7,6},{8,9},{9,8},{10,11... | collective-permute-start | bytes 3145736 | tf_op jit(solution)/shard_map/ppermute | solution.py:197
  29.1 3.7 %copy-start.10 = (s32[8,64]{1,0:T(8,128)S(1)}, s32[8,64]{1,0:T(8,128)}, u32[]{:S(2)}) copy-start(s32[8,64]{1,0:T(8,128)} %param.17) | copy-start | bytes 6148
  32.1 2.6 %copy-start.7 = (s32[8]{0:T(128)S(1)}, s32[8]{0:T(128)}, u32[]{:S(2)}) copy-start(s32[8]{0:T(128)} %param.15) | copy-start | bytes 100
  36.5 18.3 %copy-start.9 = (f32[2048]{0:T(1024)S(1)}, f32[2048]{0:T(1024)}, u32[]{:S(2)}) copy-start(f32[2048]{0:T(1024)} %param.10) | copy-start | bytes 24580
  60.6 1.5 copy-start.2
  79.2 91.2 %copy-start.8 = (s32[8]{0:T(128)S(1)}, s32[8]{0:T(128)}, u32[]{:S(2)}) copy-start(s32[8]{0:T(128)} %param.16) | copy-start | bytes 100
  79.5 92.5 %copy-start.5 = (s32[8,64,1]{2,1,0:T(8,128)S(1)}, s32[8,64,1]{2,1,0:T(8,128)}, u32[]{:S(2)}) copy-start(s32[8,64,1]{2,1,0:T(8,128)} %add_maximum_fusion) | copy-start | bytes 6148
  79.8 92.3 %copy-start.6 = (bf16[8,2,64,128]{3,2,1,0:T(8,128)(2,1)}, bf16[8,2,64,128]{3,2,1,0:T(8,128)(2,1)S(1)}, u32[]{:S(2)}) copy-start(bf16[8,2,64,128]{3,2,1,0:T(8,128)(2,1)S(1)} %maximum_bitcast_fusion.3) | copy-start | bytes 786436
  165.3 52.7 %all-to-all-start.1 = ((bf16[16,1,2,256,128]{4,3,2,1,0:T(8,128)(2,1)}), bf16[16,1,2,256,128]{4,3,2,1,0:T(8,128)(2,1)S(1)}, u32[]{:S(2)}, u32[]{:S(2)}) async-start(bf16[16,1,2,256,128]{4,3,2,1,0:T(8,128)(2,1)} %constant_dynamic-slice_fusion.2), calls=%async_computation.1 | async-start | bytes 4194304 | tf_op jit(solution)/shard_map/all_to_all | solution.py:185
  172.1 34.1 %copy-start = (bf16[1024,2048]{1,0:T(8,128)(2,1)S(1)}, bf16[1024,2048]{1,0:T(8,128)(2,1)}, u32[]{:S(2)}) copy-start(bf16[1024,2048]{1,0:T(8,128)(2,1)} %param.13) | copy-start | bytes 12582916
  208.1 4.3 %copy-start.3 = (f32[6,64,2048]{2,1,0:T(8,128)}, f32[6,64,2048]{2,1,0:T(8,128)S(1)}, u32[]{:S(2)}) copy-start(f32[6,64,2048]{2,1,0:T(8,128)S(1)} %fusion.9) | copy-start | bytes 9437188
  209.2 21.7 %collective-permute-start.1 = (bf16[6,32,2048]{2,1,0:T(8,128)(2,1)}, bf16[6,32,2048]{2,1,0:T(8,128)(2,1)}, u32[]{:S(2)}, u32[]{:S(2)}) collective-permute-start(bf16[6,32,2048]{2,1,0:T(8,128)(2,1)} %slice.166), channel_id=1, source_target_pairs={{0,1},{1,0},{2,3},{3,2},{4,5},{5,4},{6,7},{7,6},{8,9},{9,8},{10,11... | collective-permute-start | bytes 2359304 | tf_op jit(solution)/shard_map/ppermute | solution.py:263
  218.1 10.7 %copy-start.1 = (bf16[1024,2048]{1,0:T(8,128)(2,1)S(1)}, bf16[1024,2048]{1,0:T(8,128)(2,1)}, u32[]{:S(2)}) copy-start(bf16[1024,2048]{1,0:T(8,128)(2,1)} %param.13) | copy-start | bytes 12582916
  228.8 2.1 copy-start.4
  229.6 8.1 %collective-permute-start.2 = (bf16[2,32,2048]{2,1,0:T(8,128)(2,1)S(1)}, bf16[2,32,2048]{2,1,0:T(8,128)(2,1)S(1)}, u32[]{:S(2)}, u32[]{:S(2)}) collective-permute-start(bf16[2,32,2048]{2,1,0:T(8,128)(2,1)S(1)} %slice.167), channel_id=1, source_target_pairs={{0,1},{1,0},{2,3},{3,2},{4,5},{5,4},{6,7},{7,6},{8,9},{9,8},{10,11... | collective-permute-start | bytes 786440 | tf_op jit(solution)/shard_map/ppermute | solution.py:263
